TPU v7x, 256 devices: a whole 4x4x8 slice. The times are simulated.
256 devices in a mesh: tm: 32 (over z, x), head: 8 (over y, core).
Axes of the slice: x: 4, y: 4, z: 8, core: 2. Of those that a mesh axis runs over, the one named last changes fastest.
Arguments:
- query_rows: float32 [32768, 2048], P('tm', 'head'), may hold values from -0.09375 to 0.09375
- key_rows: float32 [32768, 2048], P('tm', 'head'), may hold values from -0.09375 to 0.09375
- value_rows: float32 [32768, 2048], P('tm', 'head'), may hold values from -1 to 1
- out_grad: float32 [32768, 2048], P('tm', 'head'), may hold values from -1 to 1
- level_weights: float32 [16, 32768], P(None, 'tm'), may hold values from 0.3 to 3
Outputs:
- query_grad: float32 [32768, 2048], P('tm', 'head')
- key_grad: float32 [32768, 2048], P('tm', 'head')
- value_grad: float32 [32768, 2048], P('tm', 'head')
- weight_grad: float32 [16, 32768], P(None, 'tm')
All inputs are finite; a program needn't handle non-finite values.
Results may differ from a plain program's by a relative error of at most 0.00011.
Values sent between devices are 32-bit elements; how exact they have to be, the bound alone decides.
A program may use at most 128 MiB of HBM per device.

v0:
```python
import jax
import jax.numpy as jnp
from jax import lax
from jax.experimental import pallas as pl
from jax.experimental.pallas import tpu as pltpu
from jax.sharding import PartitionSpec as P

MESH = pl.DeviceIdType.MESH
F32 = jnp.float32
BF16 = jnp.bfloat16
DK = 128
C = 128
FR = 1024
NC = FR // C
NX, NZ, NG = 4, 8, 8
HH = 2
PR = DK // NX


def nt(a, b):
    return lax.dot_general(a, b, (((1,), (1,)), ((), ())), preferred_element_type=F32)


def nn(a, b):
    return jnp.dot(a, b, preferred_element_type=F32)


def split(x):
    hi = x.astype(BF16)
    return hi, (x - hi.astype(F32)).astype(BF16)


def quads(x):
    return (x[:DK, :DK] + x[:DK, DK:]) + (x[DK:, :DK] + x[DK:, DK:])


def as_left(x):
    hi, lo = split(x)
    return jnp.concatenate([hi, lo, hi], axis=1)


def kernel(
    q_hbm, k_hbm, v_hbm, d_hbm, w_hbm, qg_hbm, kg_hbm, vg_hbm, wg_hbm,
    qin, kin, vin, din, win, qo, ko, vo, wo,
    k3, v3, q3, d3, kt, qt, qgt, levels, sch, snode, sgnode, sleft, sbd,
    a_src, a_rcv, p_rcv, b_src, b_rcv, c_src, c_rcv, w_src, w_rcv, w_fin,
    in_sem, out_sem, a_ss, a_rs, p_ss, p_rs, b_ss, b_rs, c_ss, c_rs, w_ss, w_rs, f_ss, f_rs,
):
    me = lax.axis_index("tm")
    g = lax.axis_index("head")
    x = lax.rem(me, NX)
    z = lax.div(me, NX)
    xb = (lax.rem(x, 2), lax.div(x, 2))
    zb = (lax.rem(z, 2), lax.rem(lax.div(z, 2), 2), lax.div(z, 4))
    bits = xb + zb

    def xpeer(j):
        return lax.rem(x + j, NX)

    def zpeer(j):
        return lax.rem(z + j, NZ)

    def gpeer(j):
        return lax.rem(g + j, NG)

    barrier = pltpu.get_barrier_semaphore()
    for j in range(1, NX):
        pl.semaphore_signal(barrier, 1, device_id=(z * NX + xpeer(j), g), device_id_type=MESH)
    for j in range(1, NZ):
        pl.semaphore_signal(barrier, 1, device_id=(zpeer(j) * NX + x, g), device_id_type=MESH)
    for j in range(1, NG):
        pl.semaphore_signal(barrier, 1, device_id=(me, gpeer(j)), device_id_type=MESH)

    def loads(h):
        cols = pl.ds(h * DK, DK)
        return [
            pltpu.make_async_copy(src.at[:, cols], dst.at[:, cols], in_sem.at[h, i])
            for i, (src, dst) in enumerate(((k_hbm, kin), (v_hbm, vin), (q_hbm, qin), (d_hbm, din)))
        ]

    w_load = pltpu.make_async_copy(w_hbm, win, in_sem.at[HH, 0])
    for h in range(HH):
        for copy in loads(h):
            copy.start()
        if h == 0:
            w_load.start()

    source = lax.broadcasted_iota(jnp.int32, (C, C), 0)
    target = lax.broadcasted_iota(jnp.int32, (C, C), 1)
    digits = jnp.zeros((C, C), jnp.int32)
    for k in range(7):
        apart = lax.shift_right_logical(source, k) != lax.shift_right_logical(target, k)
        digits = digits + jnp.where(apart, 1, 0)
    levels[...] = jnp.where(source <= target, digits, -1)
    sleft[...] = jnp.zeros_like(sleft)
    sgnode[...] = jnp.zeros_like(sgnode)
    w_src[...] = jnp.zeros_like(w_src)
    sbd[...] = jnp.zeros_like(sbd)

    def remote(src, dst, ss, rs, tm, head):
        return pltpu.make_async_remote_copy(
            src_ref=src, dst_ref=dst, send_sem=ss, recv_sem=rs, device_id=(tm, head), device_id_type=MESH
        )

    def a_needed(item, src_x):
        if item == 0:
            return jnp.logical_or(z < NZ - 1, src_x < 2)
        if item == 1:
            return src_x >= 2
        return zb[item - 2] == 1

    def a_send(h, item, j):
        to = xpeer(j)
        row = 0 if item == 0 else item + 1
        return remote(
            a_src.at[h, row, pl.ds(to * PR, PR), :], a_rcv.at[h, item, x],
            a_ss.at[h, item, j - 1], a_rs.at[h, item, x], z * NX + to, g,
        )

    def a_recv(h, item, j):
        come = xpeer(j)
        return remote(
            a_src.at[h, 0, pl.ds(come * PR, PR), :], a_rcv.at[h, item, come],
            a_ss.at[h, item, j - 1], a_rs.at[h, item, come], z * NX + come, g,
        )

    def p_copy(h):
        return remote(
            a_src.at[h, xb[0]], p_rcv.at[h], p_ss.at[h], p_rs.at[h], z * NX + (x + 1 - 2 * xb[0]), g
        )

    def a_start(h, item):
        @pl.when(a_needed(item, x))
        def _():
            for j in range(1, NX):
                a_send(h, item, j).start()

    def b_send(h, j):
        to = zpeer(j)
        level = (
            1
            + (lax.div(z, 2) != lax.div(to, 2)).astype(jnp.int32)
            + (lax.div(z, 4) != lax.div(to, 4)).astype(jnp.int32)
        )
        row = jnp.where(z < to, 0, level)
        return remote(
            b_src.at[h, row], b_rcv.at[h, z], b_ss.at[h, j - 1], b_rs.at[h, z], to * NX + x, g
        )

    def b_recv(h, j):
        come = zpeer(j)
        return remote(
            b_src.at[h, 0], b_rcv.at[h, come], b_ss.at[h, j - 1], b_rs.at[h, come], come * NX + x, g
        )

    def c_needed(item, dst_x):
        if item == 0:
            return dst_x >= 2
        if item == 4:
            return jnp.logical_or(z < NZ - 1, dst_x < 2)
        return zb[item - 1] == 1

    def c_row(item, dst_x):
        return 4 + jnp.where(dst_x < 2, 0, 1) if item == 4 else item

    def c_send(h, item, j):
        to = xpeer(j)
        return remote(
            c_src.at[h, c_row(item, to)], c_rcv.at[h, item, pl.ds(x * PR, PR), :],
            c_ss.at[h, item, j - 1], c_rs.at[h, item, x], z * NX + to, g,
        )

    def c_recv(h, item, j):
        come = xpeer(j)
        return remote(
            c_src.at[h, item], c_rcv.at[h, item, pl.ds(come * PR, PR), :],
            c_ss.at[h, item, j - 1], c_rs.at[h, item, come], z * NX + come, g,
        )

    def c_start(h, item):
        for j in range(1, NX):
            @pl.when(c_needed(item, xpeer(j)))
            def _():
                c_send(h, item, j).start()

        @pl.when(c_needed(item, x))
        def _():
            c_rcv[h, item, pl.ds(x * PR, PR), :] = c_src[h, c_row(item, x)]

    def w_send(j):
        to = gpeer(j)
        return remote(w_src.at[to], w_rcv.at[g], w_ss.at[j - 1], w_rs.at[g], me, to)

    def w_recv(j):
        come = gpeer(j)
        return remote(w_src.at[come], w_rcv.at[come], w_ss.at[j - 1], w_rs.at[come], me, come)

    def f_send(j):
        to = gpeer(j)
        return remote(w_fin.at[g], w_fin.at[g], f_ss.at[j - 1], f_rs.at[g], me, to)

    def f_recv(j):
        come = gpeer(j)
        return remote(w_fin.at[come], w_fin.at[come], f_ss.at[j - 1], f_rs.at[come], me, come)

    def prepare(h):
        cols = pl.ds(h * DK, DK)
        copies = loads(h)
        copies[0].wait()
        copies[1].wait()

        def keys(c, carry):
            r = pl.ds(pl.multiple_of(c * C, C), C)
            key = kin[r, cols]
            hi, lo = split(key)
            k3[h, r, :] = jnp.concatenate([hi, lo, hi], axis=1)
            vhi, vlo = split(vin[r, cols])
            v3[h, r, :] = jnp.concatenate([vhi, vlo, vhi], axis=1)
            thi, tlo = split(key.T)
            kt[h, 0:DK, r] = thi
            kt[h, DK : 2 * DK, r] = tlo
            both = nn(jnp.concatenate([thi, tlo], axis=0), jnp.concatenate([vhi, vlo], axis=1))
            sch[c] = quads(both)
            return carry

        lax.fori_loop(0, NC, keys, 0)
        pairs = [sch[2 * i] + sch[2 * i + 1] for i in range(4)]
        for i in range(4):
            snode[h, i] = as_left(sch[2 * i])
        snode[h, 4] = as_left(pairs[0])
        snode[h, 5] = as_left(pairs[2])
        half = pairs[0] + pairs[1]
        snode[h, 6] = as_left(half)
        a_src[h, 0] = half + (pairs[2] + pairs[3])
        copies[2].wait()
        copies[3].wait()

        def queries(c, carry):
            r = pl.ds(pl.multiple_of(c * C, C), C)
            query = qin[r, cols]
            hi, lo = split(query)
            q3[h, r, :] = jnp.concatenate([hi, hi, lo], axis=1)
            dhi, dlo = split(din[r, cols])
            d3[h, r, :] = jnp.concatenate([dhi, dhi, dlo], axis=1)
            qt[h, :, r] = query.T
            return carry

        lax.fori_loop(0, NC, queries, 0)

    def cotangent(h, level):
        @pl.when(bits[level - 1] == 1)
        def _():
            hi, lo = split(qt[h] * win[10 + level : 11 + level, :])
            a_src[h, level] = quads(nn(jnp.concatenate([hi, lo], axis=0), d3[h, :, DK : 3 * DK]))

    for h in range(HH):
        prepare(h)
        if h == 0:
            w_load.wait()
            pl.semaphore_wait(barrier, NX + NZ + NG - 3)
        a_start(h, 0)
        for level in (2, 3, 4, 5):
            cotangent(h, level)
            a_start(h, level - 1)
        cotangent(h, 1)
        p_copy(h).start()

    def chunk(c, carry):
        r = pl.ds(pl.multiple_of(c * C, C), C)
        weights = win[:, r]
        level = levels[...]
        mixing = jnp.zeros((C, C), F32)
        for k in range(8):
            mixing = jnp.where(level == k, weights[k : k + 1, :], mixing)
        product = jnp.zeros((C, C), F32)
        for h in range(HH):
            scores = nt(k3[h, r, :], q3[h, r, :])
            backs = nt(v3[h, r, :], d3[h, r, :])
            product = product + scores * backs
            bhi, blo = split(backs * mixing)
            shi, slo = split(scores * mixing)
            q2 = q3[h, r, DK : 3 * DK]
            d2 = d3[h, r, DK : 3 * DK]
            key = nn(jnp.concatenate([bhi, blo], axis=1), jnp.concatenate([q2, q2], axis=0))
            val = nn(jnp.concatenate([shi, slo], axis=1), jnp.concatenate([d2, d2], axis=0))
            ko[r, h * DK : (h + 1) * DK] = key[:, :DK] + key[:, DK:]
            vo[r, h * DK : (h + 1) * DK] = val[:, :DK] + val[:, DK:]
            thi = kt[h, 0:DK, r]
            tlo = kt[h, DK : 2 * DK, r]
            qgt[h, :, r] = nn(
                jnp.concatenate([thi, tlo, thi], axis=1), jnp.concatenate([bhi, bhi, blo], axis=0)
            )
        rows = [
            jnp.sum(jnp.where(level == k, product, F32(0.0)), axis=0, keepdims=True) for k in range(8)
        ]
        w_src[c, 0:8, :] = jnp.concatenate(rows, axis=0)
        for k, (bit, node) in enumerate(
            (
                (lax.rem(c, 2), lax.div(c, 2)),
                (lax.rem(lax.div(c, 2), 2), 4 + lax.div(c, 4)),
                (lax.div(c, 4), 6),
            )
        ):
            @pl.when(bit == 1)
            def _():
                weight = win[8 + k : 9 + k, r]
                total = jnp.zeros((1, C), F32)
                for h in range(HH):
                    along = nt(snode[h, node], d3[h, r, :])
                    query = qt[h, :, r]
                    qgt[h, :, r] += weight * along
                    total = total + jnp.sum(query * along, axis=0, keepdims=True)
                    hi, lo = split(query * weight)
                    sgnode[h, node] += quads(
                        nn(jnp.concatenate([hi, lo], axis=0), d3[h, r, DK : 3 * DK])
                    )
                w_src[c, 8 + k : 9 + k, :] = total
        return carry

    def a_end(h):
        for item in range(5):
            for j in range(1, NX):
                @pl.when(a_needed(item, xpeer(j)))
                def _():
                    a_recv(h, item, j).wait_recv()

            @pl.when(a_needed(item, x))
            def _():
                row = 0 if item == 0 else item + 1
                a_rcv[h, item, x] = a_src[h, row, pl.ds(x * PR, PR), :]

        @pl.when(z < NZ - 1)
        def _():
            b_src[h, 0] = (a_rcv[h, 0, 0] + a_rcv[h, 0, 1]) + (a_rcv[h, 0, 2] + a_rcv[h, 0, 3])

        for i in range(3):
            @pl.when(zb[i] == 1)
            def _():
                b_src[h, 1 + i] = (a_rcv[h, 2 + i, 0] + a_rcv[h, 2 + i, 1]) + (
                    a_rcv[h, 2 + i, 2] + a_rcv[h, 2 + i, 3]
                )

        for j in (4, 3, 5, 2, 6, 1, 7):
            b_send(h, j).start()
        c_src[h, 0] = a_rcv[h, 0, 0] + a_rcv[h, 0, 1]
        c_start(h, 0)

    def b_end(h):
        for j in range(1, NZ):
            b_recv(h, j).wait_recv()

        @pl.when(zb[0] == 1)
        def _():
            c_src[h, 1] = b_rcv[h, z - 1]

        @pl.when(zb[1] == 1)
        def _():
            first = 2 * lax.div(z, 2) - 2
            c_src[h, 2] = b_rcv[h, first] + b_rcv[h, first + 1]

        @pl.when(zb[2] == 1)
        def _():
            c_src[h, 3] = (b_rcv[h, 0] + b_rcv[h, 1]) + (b_rcv[h, 2] + b_rcv[h, 3])

        c_src[h, 5] = jnp.zeros((PR, DK), F32)
        for other in range(1, NZ):
            @pl.when(other > z)
            def _():
                c_src[h, 5] += b_rcv[h, other]
        c_src[h, 4] = c_src[h, 5] + (a_rcv[h, 1, 2] + a_rcv[h, 1, 3])
        for item in range(1, 5):
            c_start(h, item)

    def near_states(h):
        p_copy(h).wait_recv()
        for j in range(1, NX):
            @pl.when(jnp.logical_and(c_needed(0, x), True))
            def _():
                c_recv(h, 0, j).wait_recv()

        @pl.when(xb[0] == 1)
        def _():
            sleft[h, 0:DK, :] = as_left(p_rcv[h])

        @pl.when(xb[0] == 0)
        def _():
            sbd[h] += p_rcv[h]

        @pl.when(xb[1] == 1)
        def _():
            sleft[h, DK : 2 * DK, :] = as_left(c_rcv[h, 0])

    def far_states(h):
        for item in range(1, 5):
            @pl.when(c_needed(item, x))
            def _():
                for j in range(1, NX):
                    c_recv(h, item, j).wait_recv()
                if item < 4:
                    sleft[h, (item + 1) * DK : (item + 2) * DK, :] = as_left(c_rcv[h, item])
                else:
                    sbd[h] += c_rcv[h, 4]

    def coarse(h, first, count):
        def tile(i, carry):
            r = pl.ds(pl.multiple_of(i * 2 * C, 2 * C), 2 * C)
            along = nt(sleft[h, first * DK : (first + count) * DK, :], d3[h, r, :])
            query = qt[h, :, r]
            total = qgt[h, :, r]
            for n in range(count):
                row = 11 + first + n
                part = along[n * DK : (n + 1) * DK]
                total = total + win[row : row + 1, r] * part
                terms = jnp.sum(query * part, axis=0, keepdims=True)
                w_src[2 * i, row : row + 1, :] += terms[:, :C]
                w_src[2 * i + 1, row : row + 1, :] += terms[:, C:]
            qgt[h, :, r] = total
            return carry

        lax.fori_loop(0, FR // (2 * C), tile, 0)

    def q_finish(h):
        def step(c, carry):
            r = pl.ds(pl.multiple_of(c * C, C), C)
            qo[r, h * DK : (h + 1) * DK] = qgt[h, :, r].T
            return carry

        lax.fori_loop(0, NC, step, 0)

    def kv_finish(h):
        cols = slice(h * DK, (h + 1) * DK)
        base = sbd[h]
        for c in range(NC):
            r = pl.ds(c * C, C)
            back = base
            if c % 2 == 0:
                back = back + sgnode[h, c // 2]
            if (c // 2) % 2 == 0:
                back = back + sgnode[h, 4 + c // 4]
            if c < 4:
                back = back + sgnode[h, 6]
            hi, lo = split(back)
            ko[r, cols] += nt(v3[h, r, :], jnp.concatenate([hi, hi, lo], axis=1))
            wide = jnp.concatenate([hi, lo], axis=1)
            val = nn(k3[h, r, 0 : 2 * DK], jnp.concatenate([wide, wide], axis=0))
            vo[r, cols] += val[:, :DK] + val[:, DK:]

    def out_copy(i, src, dst, h):
        cols = pl.ds(h * DK, DK)
        return pltpu.make_async_copy(src.at[:, cols], dst.at[:, cols], out_sem.at[h, i])

    lax.fori_loop(0, 2, chunk, 0)
    a_end(0)
    lax.fori_loop(2, 4, chunk, 0)
    a_end(1)
    lax.fori_loop(4, 6, chunk, 0)
    b_end(0)
    lax.fori_loop(6, 8, chunk, 0)
    b_end(1)
    near_states(0)
    coarse(0, 0, 2)
    near_states(1)
    coarse(1, 0, 2)
    far_states(0)
    coarse(0, 2, 3)
    q_finish(0)
    out_copy(0, qo, qg_hbm, 0).start()
    kv_finish(0)
    out_copy(1, ko, kg_hbm, 0).start()
    out_copy(2, vo, vg_hbm, 0).start()
    far_states(1)
    coarse(1, 2, 3)
    for j in range(1, NG):
        w_send(j).start()
    q_finish(1)
    out_copy(0, qo, qg_hbm, 1).start()
    w_rcv[g] = w_src[g]
    for j in range(1, NG):
        w_recv(j).wait_recv()
    total = w_rcv[0]
    for i in range(1, NG):
        total = total + w_rcv[i]
    w_fin[g] = total
    for j in range(1, NG):
        f_send(j).start()
    kv_finish(1)
    out_copy(1, ko, kg_hbm, 1).start()
    out_copy(2, vo, vg_hbm, 1).start()
    for j in range(1, NG):
        f_recv(j).wait_recv()
    for i in range(NG):
        wo[:, i * C : (i + 1) * C] = w_fin[i]
    w_out = pltpu.make_async_copy(wo, wg_hbm, out_sem.at[HH, 0])
    w_out.start()

    for h in range(HH):
        for item in range(5):
            @pl.when(a_needed(item, x))
            def _():
                for j in range(1, NX):
                    a_send(h, item, j).wait_send()
            for j in range(1, NX):
                @pl.when(c_needed(item, xpeer(j)))
                def _():
                    c_send(h, item, j).wait_send()
        p_copy(h).wait_send()
        for j in range(1, NZ):
            b_send(h, j).wait_send()
    for j in range(1, NG):
        w_send(j).wait_send()
        f_send(j).wait_send()
    for h in range(HH):
        out_copy(0, qo, qg_hbm, h).wait()
        out_copy(1, ko, kg_hbm, h).wait()
        out_copy(2, vo, vg_hbm, h).wait()
    w_out.wait()


def local(query_rows, key_rows, value_rows, out_grad, level_weights):
    rows = (FR, HH * DK)
    dma = pltpu.SemaphoreType.DMA
    whole = jax.ShapeDtypeStruct(rows, F32)
    anywhere = pl.BlockSpec(memory_space=pl.ANY)
    wide = (HH, FR, 3 * DK)
    return pl.pallas_call(
        kernel,
        out_shape=(whole, whole, whole, jax.ShapeDtypeStruct((16, FR), F32)),
        in_specs=[anywhere] * 5,
        out_specs=(anywhere,) * 4,
        scratch_shapes=[
            pltpu.VMEM(rows, F32), pltpu.VMEM(rows, F32), pltpu.VMEM(rows, F32), pltpu.VMEM(rows, F32),
            pltpu.VMEM((16, FR), F32),
            pltpu.VMEM(rows, F32), pltpu.VMEM(rows, F32), pltpu.VMEM(rows, F32),
            pltpu.VMEM((16, FR), F32),
            pltpu.VMEM(wide, BF16), pltpu.VMEM(wide, BF16), pltpu.VMEM(wide, BF16), pltpu.VMEM(wide, BF16),
            pltpu.VMEM((HH, 2 * DK, FR), BF16),
            pltpu.VMEM((HH, DK, FR), F32),
            pltpu.VMEM((HH, DK, FR), F32),
            pltpu.VMEM((C, C), jnp.int32),
            pltpu.VMEM((NC, DK, DK), F32),
            pltpu.VMEM((HH, 7, DK, 3 * DK), BF16),
            pltpu.VMEM((HH, 7, DK, DK), F32),
            pltpu.VMEM((HH, 5 * DK, 3 * DK), BF16),
            pltpu.VMEM((HH, DK, DK), F32),
            pltpu.VMEM((HH, 6, DK, DK), F32),
            pltpu.VMEM((HH, 5, NX, PR, DK), F32),
            pltpu.VMEM((HH, DK, DK), F32),
            pltpu.VMEM((HH, 4, PR, DK), F32),
            pltpu.VMEM((HH, NZ, PR, DK), F32),
            pltpu.VMEM((HH, 6, PR, DK), F32),
            pltpu.VMEM((HH, 5, DK, DK), F32),
            pltpu.VMEM((NC, 16, C), F32),
            pltpu.VMEM((NG, 16, C), F32),
            pltpu.VMEM((NG, 16, C), F32),
            dma((HH + 1, 4)), dma((HH + 1, 3)),
            dma((HH, 5, NX - 1)), dma((HH, 5, NX)),
            dma((HH,)), dma((HH,)),
            dma((HH, NZ - 1)), dma((HH, NZ)),
            dma((HH, 5, NX - 1)), dma((HH, 5, NX)),
            dma((NG - 1,)), dma((NG,)),
            dma((NG - 1,)), dma((NG,)),
        ],
        compiler_params=pltpu.CompilerParams(
            collective_id=0, has_side_effects=True, vmem_limit_bytes=48 * 1024 * 1024
        ),
        name="tree_backward",
    )(query_rows, key_rows, value_rows, out_grad, level_weights)


def solution(mesh):
    in_specs = (P("tm", "head"), P("tm", "head"), P("tm", "head"), P("tm", "head"), P(None, "tm"))
    out_specs = (P("tm", "head"), P("tm", "head"), P("tm", "head"), P(None, "tm"))
    return jax.shard_map(local, mesh=mesh, in_specs=in_specs, out_specs=out_specs, check_vma=False)
```

profile of v0, /device:TPU:1, one launch (start us, length us, event | category | flops | bytes accessed | tf_op | source)
XLA Modules:
  0.0 49.6 jit_solution(9524300524357466145)
XLA Ops:
  0.6 0.0 copy-start
  0.6 1.2 %copy-done = f32[1024,256]{1,0:T(8,128)S(1)} copy-done((f32[1024,256]{1,0:T(8,128)S(1)}, f32[1024,256]{1,0:T(8,128)}, u32[]{:S(2)}) %copy-start) | copy-done | bytes 1048600
  1.9 0.0 copy-start.1
  1.9 1.2 %copy-done.1 = f32[1024,256]{1,0:T(8,128)S(1)} copy-done((f32[1024,256]{1,0:T(8,128)S(1)}, f32[1024,256]{1,0:T(8,128)}, u32[]{:S(2)}) %copy-start.1) | copy-done | bytes 1048600
  3.1 0.0 copy-start.2
  3.1 0.8 %copy-done.2 = f32[16,1024]{1,0:T(8,128)S(1)} copy-done((f32[16,1024]{1,0:T(8,128)S(1)}, f32[16,1024]{1,0:T(8,128)}, u32[]{:S(2)}) %copy-start.2) | copy-done | bytes 65560
  3.9 42.1 %tree_backward.1 = (f32[1024,256]{1,0:T(8,128)S(1)}, f32[1024,256]{1,0:T(8,128)S(1)}, f32[1024,256]{1,0:T(8,128)S(1)}, f32[16,1024]{1,0:T(8,128)S(1)}) custom-call(f32[1024,256]{1,0:T(8,128)S(1)} %copy-done, f32[1024,256]{1,0:T(8,128)S(1)} %copy-done.1, f32[1024,256]{1,0:T(8,128)} %v_hbm.1, f32[1024,256]{1,0:T(8,128)} %d_hbm.1, f32[16,1024]{1,0:T(8,128)S(1)} %copy-done.2), custom_call_target="tpu_custom_call" | custom-call | tf_op jit(solution)/shard_map/tree_backward/pallas_call | solution.py:525
  46.0 1.0 %copy.13 = f32[1024,256]{1,0:T(8,128)} copy(f32[1024,256]{1,0:T(8,128)S(1)} %get-tuple-element.8) | data formatting | bytes 2097152
  47.0 1.0 %copy.14 = f32[1024,256]{1,0:T(8,128)} copy(f32[1024,256]{1,0:T(8,128)S(1)} %get-tuple-element.9) | data formatting | bytes 2097152
  48.0 1.0 %copy.15 = f32[1024,256]{1,0:T(8,128)} copy(f32[1024,256]{1,0:T(8,128)S(1)} %get-tuple-element.10) | data formatting | bytes 2097152
  49.0 0.6 %copy.16 = f32[16,1024]{1,0:T(8,128)} copy(f32[16,1024]{1,0:T(8,128)S(1)} %get-tuple-element.11) | data formatting | bytes 131072
Async XLA Ops:
  0.6 1.2 %copy-start = (f32[1024,256]{1,0:T(8,128)S(1)}, f32[1024,256]{1,0:T(8,128)}, u32[]{:S(2)}) copy-start(f32[1024,256]{1,0:T(8,128)} %q_hbm.1) | copy-start | bytes 3145732
  1.9 1.2 %copy-start.1 = (f32[1024,256]{1,0:T(8,128)S(1)}, f32[1024,256]{1,0:T(8,128)}, u32[]{:S(2)}) copy-start(f32[1024,256]{1,0:T(8,128)} %k_hbm.1) | copy-start | bytes 3145732
  3.1 0.8 %copy-start.2 = (f32[16,1024]{1,0:T(8,128)S(1)}, f32[16,1024]{1,0:T(8,128)}, u32[]{:S(2)}) copy-start(f32[16,1024]{1,0:T(8,128)} %w_hbm.1) | copy-start | bytes 196612
where the time goes:
time: 49.8 us; the launch traced here: 49.6 us
  Pallas kernels  42.1 us (85%)
  local copies, waits for them, and re-layouts  6.82 us (14%)
  between operations  0.65 us (1%)
    pallas_call x1, Pallas kernels, local(): pl.pallas_call(kernel, out_shape=(whole, whole, whole, jax.ShapeDtypeStru...  42.1 us
    unnamed x10, local copies, waits for them, and re-layouts  6.82 us

commit v1 on v0

v1 whole, which is shorter than its diff:
```python
import jax
import jax.numpy as jnp
from jax import lax
from jax.experimental import pallas as pl
from jax.experimental.pallas import tpu as pltpu
from jax.sharding import PartitionSpec as P

MESH = pl.DeviceIdType.MESH
F32 = jnp.float32
BF16 = jnp.bfloat16
DK = 128
C = 128
FR = 1024
NC = FR // C
NX, NZ, NG = 4, 8, 8
HH = 2
PR = DK // NX


def nt(a, b):
    return lax.dot_general(a, b, (((1,), (1,)), ((), ())), preferred_element_type=F32)


def nn(a, b):
    return jnp.dot(a, b, preferred_element_type=F32)


def split(x):
    hi = x.astype(BF16)
    return hi, (x - hi.astype(F32)).astype(BF16)


def quads(x):
    return (x[:DK, :DK] + x[:DK, DK:]) + (x[DK:, :DK] + x[DK:, DK:])


def as_left(x):
    hi, lo = split(x)
    return jnp.concatenate([hi, lo, hi], axis=1)


def kernel(
    q_hbm, k_hbm, v_hbm, d_hbm, w_hbm, qg_hbm, kg_hbm, vg_hbm, wg_hbm,
    qin, kin, vin, din, win, qo, ko, vo, wo,
    k3, v3, q3, d3, kt, qt, qgt, levels, snode, sgnode, sleft, sbd,
    a_src, a_rcv, p_rcv, b_src, b_rcv, c_src, c_rcv, w_src, w_rcv, w_fin, l_src, l_rcv,
    in_sem, out_sem, a_ss, a_rs, p_ss, p_rs, b_ss, b_rs, c_ss, c_rs, w_ss, w_rs, f_ss, f_rs, l_ss, l_rs,
):
    me = lax.axis_index("tm")
    g = lax.axis_index("head")
    x = lax.rem(me, NX)
    z = lax.div(me, NX)
    xb = (lax.rem(x, 2), lax.div(x, 2))
    zb = (lax.rem(z, 2), lax.rem(lax.div(z, 2), 2), lax.div(z, 4))
    bits = xb + zb

    def xpeer(j):
        return lax.rem(x + j, NX)

    def zpeer(j):
        return lax.rem(z + j, NZ)

    def gpeer(j):
        return lax.rem(g + j, NG)

    barrier = pltpu.get_barrier_semaphore()
    for j in range(1, NX):
        pl.semaphore_signal(barrier, 1, device_id=(z * NX + xpeer(j), g), device_id_type=MESH)
    for j in range(1, NZ):
        pl.semaphore_signal(barrier, 1, device_id=(zpeer(j) * NX + x, g), device_id_type=MESH)
    for j in range(1, NG):
        pl.semaphore_signal(barrier, 1, device_id=(me, gpeer(j)), device_id_type=MESH)

    def load(i, h):
        src, dst = ((k_hbm, kin), (v_hbm, vin), (q_hbm, qin), (d_hbm, din))[i]
        cols = pl.ds(h * DK, DK)
        return pltpu.make_async_copy(src.at[:, cols], dst.at[:, cols], in_sem.at[h, i])

    w_load = pltpu.make_async_copy(w_hbm, win, in_sem.at[HH, 0])
    for i in (0, 1):
        for h in range(HH):
            load(i, h).start()
    w_load.start()
    for i in (2, 3):
        for h in range(HH):
            load(i, h).start()

    source = lax.broadcasted_iota(jnp.int32, (C, C), 0)
    target = lax.broadcasted_iota(jnp.int32, (C, C), 1)
    digits = jnp.zeros((C, C), jnp.int32)
    for k in range(7):
        apart = lax.shift_right_logical(source, k) != lax.shift_right_logical(target, k)
        digits = digits + jnp.where(apart, 1, 0)
    levels[...] = jnp.where(source <= target, digits, -1)
    sleft[...] = jnp.zeros_like(sleft)
    w_src[...] = jnp.zeros_like(w_src)
    sbd[...] = jnp.zeros_like(sbd)

    def remote(src, dst, ss, rs, tm, head):
        return pltpu.make_async_remote_copy(
            src_ref=src, dst_ref=dst, send_sem=ss, recv_sem=rs, device_id=(tm, head), device_id_type=MESH
        )

    def a_needed(item, src_x):
        if item == 0:
            return jnp.logical_or(z < NZ - 1, src_x < 2)
        if item == 1:
            return src_x >= 2
        return zb[item - 2] == 1

    def a_piece(item, of):
        return a_src.at[0 if item == 0 else item + 1, :, pl.ds(of * PR, PR), :]

    def a_send(item, j):
        to = xpeer(j)
        return remote(
            a_piece(item, to), a_rcv.at[item, x], a_ss.at[item, j - 1], a_rs.at[item, x], z * NX + to, g
        )

    def a_recv(item, j):
        come = xpeer(j)
        return remote(
            a_piece(item, come), a_rcv.at[item, come], a_ss.at[item, j - 1], a_rs.at[item, come],
            z * NX + come, g,
        )

    def p_copy():
        return remote(a_src.at[xb[0]], p_rcv, p_ss, p_rs, z * NX + (x + 1 - 2 * xb[0]), g)

    def a_start(item):
        @pl.when(a_needed(item, x))
        def _():
            for j in range(1, NX):
                a_send(item, j).start()
            a_rcv[item, x] = a_src[0 if item == 0 else item + 1, :, pl.ds(x * PR, PR), :]

    def a_wait(item):
        for j in range(1, NX):
            @pl.when(a_needed(item, xpeer(j)))
            def _():
                a_recv(item, j).wait_recv()

    def a_total(item):
        return (a_rcv[item, 0] + a_rcv[item, 1]) + (a_rcv[item, 2] + a_rcv[item, 3])

    def b_send(to, row):
        return remote(b_src.at[row], b_rcv.at[z], b_ss.at[to], b_rs.at[z], to * NX + x, g)

    def b_recv(come):
        return remote(b_src.at[0], b_rcv.at[come], b_ss.at[come], b_rs.at[come], come * NX + x, g)

    def b_level(to):
        return (
            1
            + (lax.div(z, 2) != lax.div(to, 2)).astype(jnp.int32)
            + (lax.div(z, 4) != lax.div(to, 4)).astype(jnp.int32)
        )

    def c_needed(item, dst_x):
        if item == 0:
            return dst_x >= 2
        if item == 4:
            return jnp.logical_or(z < NZ - 1, dst_x < 2)
        return zb[item - 1] == 1

    def c_row(item, dst_x):
        return 4 + jnp.where(dst_x < 2, 0, 1) if item == 4 else item

    def c_send(item, j):
        to = xpeer(j)
        return remote(
            c_src.at[c_row(item, to)], c_rcv.at[item, :, pl.ds(x * PR, PR), :],
            c_ss.at[item, j - 1], c_rs.at[item, x], z * NX + to, g,
        )

    def c_recv(item, j):
        come = xpeer(j)
        return remote(
            c_src.at[item], c_rcv.at[item, :, pl.ds(come * PR, PR), :],
            c_ss.at[item, j - 1], c_rs.at[item, come], z * NX + come, g,
        )

    def c_start(item):
        for j in range(1, NX):
            @pl.when(c_needed(item, xpeer(j)))
            def _():
                c_send(item, j).start()

        @pl.when(c_needed(item, x))
        def _():
            c_rcv[item, :, pl.ds(x * PR, PR), :] = c_src[c_row(item, x)]

    def w_send(j):
        to = gpeer(j)
        return remote(w_src.at[to], w_rcv.at[g], w_ss.at[j - 1], w_rs.at[g], me, to)

    def w_recv(j):
        come = gpeer(j)
        return remote(w_src.at[come], w_rcv.at[come], w_ss.at[j - 1], w_rs.at[come], me, come)

    def f_send(j):
        to = gpeer(j)
        return remote(w_fin.at[g], w_fin.at[g], f_ss.at[j - 1], f_rs.at[g], me, to)

    def f_recv(j):
        come = gpeer(j)
        return remote(w_fin.at[come], w_fin.at[come], f_ss.at[j - 1], f_rs.at[come], me, come)

    def l_send(j):
        to = gpeer(j)
        return remote(l_src, l_rcv.at[g], l_ss.at[j - 1], l_rs.at[g], me, to)

    def l_recv(j):
        come = gpeer(j)
        return remote(l_src, l_rcv.at[come], l_ss.at[j - 1], l_rs.at[come], me, come)

    def keys(h):
        cols = slice(h * DK, (h + 1) * DK)
        load(0, h).wait()
        load(1, h).wait()
        states = []
        for c in range(NC):
            r = slice(c * C, (c + 1) * C)
            key = kin[r, cols]
            hi, lo = split(key)
            k3[h, r, :] = jnp.concatenate([hi, lo, hi], axis=1)
            vhi, vlo = split(vin[r, cols])
            v3[h, r, :] = jnp.concatenate([vhi, vlo, vhi], axis=1)
            thi, tlo = split(key.T)
            kt[h, 0:DK, r] = thi
            kt[h, DK : 2 * DK, r] = tlo
            both = nn(jnp.concatenate([thi, tlo], axis=0), jnp.concatenate([vhi, vlo], axis=1))
            states.append(quads(both))
        pairs = [states[2 * i] + states[2 * i + 1] for i in range(4)]
        half = pairs[0] + pairs[1]
        a_src[0, h] = half + (pairs[2] + pairs[3])
        for i in range(4):
            snode[h, i] = as_left(states[2 * i])
        snode[h, 4] = as_left(pairs[0])
        snode[h, 5] = as_left(pairs[2])
        snode[h, 6] = as_left(half)

    def queries(h):
        cols = slice(h * DK, (h + 1) * DK)
        load(2, h).wait()
        load(3, h).wait()
        for c in range(NC):
            r = slice(c * C, (c + 1) * C)
            query = qin[r, cols]
            hi, lo = split(query)
            q3[h, r, :] = jnp.concatenate([hi, hi, lo], axis=1)
            dhi, dlo = split(din[r, cols])
            d3[h, r, :] = jnp.concatenate([dhi, dhi, dlo], axis=1)
            qt[h, :, r] = query.T

    def cotangent(level):
        @pl.when(bits[level - 1] == 1)
        def _():
            for h in range(HH):
                hi, lo = split(qt[h] * win[10 + level : 11 + level, :])
                a_src[level, h] = quads(nn(jnp.concatenate([hi, lo], axis=0), d3[h, :, DK : 3 * DK]))

    def fine(i):
        wide = slice(2 * i * C, 2 * (i + 1) * C)
        level = levels[...]
        along_of = []
        for h in range(HH):
            nodes = ([4 + i // 2] if i % 2 else []) + ([6] if i >= 2 else [])
            parts = [(8, i, slice((2 * i + 1) * C, (2 * i + 2) * C))]
            parts += [(9 if node < 6 else 10, node, wide) for node in nodes]
            along_of.append([(lev, node, r, nt(snode[h, node], d3[h, r, :])) for lev, node, r in parts])
        q_parts = [[], []]
        for sub in range(2):
            c = 2 * i + sub
            r = slice(c * C, (c + 1) * C)
            weights = win[:, r]
            mixing = jnp.zeros((C, C), F32)
            for k in range(8):
                mixing = jnp.where(level == k, weights[k : k + 1, :], mixing)
            product = jnp.zeros((C, C), F32)
            for h in range(HH):
                scores = nt(k3[h, r, :], q3[h, r, :])
                backs = nt(v3[h, r, :], d3[h, r, :])
                product = product + scores * backs
                bhi, blo = split(backs * mixing)
                shi, slo = split(scores * mixing)
                q2 = q3[h, r, DK : 3 * DK]
                d2 = d3[h, r, DK : 3 * DK]
                key = nn(jnp.concatenate([bhi, blo], axis=1), jnp.concatenate([q2, q2], axis=0))
                val = nn(jnp.concatenate([shi, slo], axis=1), jnp.concatenate([d2, d2], axis=0))
                ko[r, h * DK : (h + 1) * DK] = key[:, :DK] + key[:, DK:]
                vo[r, h * DK : (h + 1) * DK] = val[:, :DK] + val[:, DK:]
                thi = kt[h, 0:DK, r]
                tlo = kt[h, DK : 2 * DK, r]
                q_parts[h].append(
                    nn(jnp.concatenate([thi, tlo, thi], axis=1), jnp.concatenate([bhi, bhi, blo], axis=0))
                )
            rows = [
                jnp.sum(jnp.where(level == k, product, F32(0.0)), axis=0, keepdims=True) for k in range(8)
            ]
            w_src[c, 0:8, :] = jnp.concatenate(rows, axis=0)
        terms = {}
        for h in range(HH):
            for lev, node, r, along in along_of[h]:
                weight = win[lev : lev + 1, r]
                query = qt[h, :, r]
                add = weight * along
                if lev == 8:
                    q_parts[h][1] = q_parts[h][1] + add
                else:
                    q_parts[h][0] = q_parts[h][0] + add[:, :C]
                    q_parts[h][1] = q_parts[h][1] + add[:, C:]
                term = jnp.sum(query * along, axis=0, keepdims=True)
                terms[lev] = terms[lev] + term if h else term
                hi, lo = split(query * weight)
                grad = quads(nn(jnp.concatenate([hi, lo], axis=0), d3[h, r, DK : 3 * DK]))
                if lev == 10 and i == 3:
                    sgnode[h, node] += grad
                else:
                    sgnode[h, node] = grad
            for sub in range(2):
                c = 2 * i + sub
                qgt[h, :, c * C : (c + 1) * C] = q_parts[h][sub]
        for lev, term in terms.items():
            if lev == 8:
                w_src[2 * i + 1, 8:9, :] = term
            else:
                w_src[2 * i, lev : lev + 1, :] = term[:, :C]
                w_src[2 * i + 1, lev : lev + 1, :] = term[:, C:]

    def states_end():
        a_wait(0)

        @pl.when(z < NZ - 1)
        def _():
            b_src[0] = a_total(0)

        for to in (7, 6, 5, 4, 3, 2, 1):
            @pl.when(z < to)
            def _():
                b_send(to, 0).start()

        c_src[0] = a_rcv[0, 0] + a_rcv[0, 1]
        c_start(0)

    def cotangents_end():
        for item in range(1, 5):
            a_wait(item)
        for i in range(3):
            @pl.when(zb[i] == 1)
            def _():
                b_src[1 + i] = a_total(2 + i)

        for to in range(NZ - 1):
            @pl.when(z > to)
            def _():
                b_send(to, b_level(to)).start()

    def states_on(item):
        @pl.when(zb[item - 1] == 1)
        def _():
            count = 1 << (item - 1)
            first = lax.div(z, count) * count - count
            for i in range(count):
                b_recv(first + i).wait_recv()
            total = b_rcv[first]
            for i in range(1, count):
                total = total + b_rcv[first + i]
            c_src[item] = total

        c_start(item)

    def cotangents_on():
        c_src[5] = jnp.zeros((HH, PR, DK), F32)
        for other in range(1, NZ):
            @pl.when(other > z)
            def _():
                b_recv(other).wait_recv()
                c_src[5] += b_rcv[other]
        c_src[4] = c_src[5] + (a_rcv[1, 2] + a_rcv[1, 3])
        c_start(4)

    def near_states():
        p_copy().wait_recv()

        @pl.when(xb[0] == 1)
        def _():
            for h in range(HH):
                sleft[h, 0:DK, :] = as_left(p_rcv[h])

        @pl.when(xb[0] == 0)
        def _():
            sbd[...] = p_rcv[...]

        @pl.when(xb[1] == 1)
        def _():
            for j in range(1, NX):
                c_recv(0, j).wait_recv()
            for h in range(HH):
                sleft[h, DK : 2 * DK, :] = as_left(c_rcv[0, h])

    def far_states(item):
        @pl.when(c_needed(item, x))
        def _():
            for j in range(1, NX):
                c_recv(item, j).wait_recv()
            if item == 4:
                sbd[...] += c_rcv[4]
            else:
                for h in range(HH):
                    sleft[h, (item + 1) * DK : (item + 2) * DK, :] = as_left(c_rcv[item, h])

    def coarse(first, count):
        for i in range(FR // (2 * C)):
            r = slice(i * 2 * C, (i + 1) * 2 * C)
            terms = [jnp.zeros((1, 2 * C), F32)] * count
            for h in range(HH):
                along = nt(sleft[h, first * DK : (first + count) * DK, :], d3[h, r, :])
                query = qt[h, :, r]
                total = qgt[h, :, r]
                for n in range(count):
                    part = along[n * DK : (n + 1) * DK]
                    total = total + win[11 + first + n : 12 + first + n, r] * part
                    terms[n] = terms[n] + jnp.sum(query * part, axis=0, keepdims=True)
                qgt[h, :, r] = total
            for n in range(count):
                row = 11 + first + n
                for sub in range(2):
                    part = terms[n][:, sub * C : (sub + 1) * C]
                    if row < 13:
                        w_src[2 * i + sub, row : row + 1, :] = part
                    else:
                        l_src[row - 13, 2 * i + sub : 2 * i + sub + 1, :] = part

    def q_finish(h):
        for c in range(NC):
            r = slice(c * C, (c + 1) * C)
            qo[r, h * DK : (h + 1) * DK] = qgt[h, :, r].T
        out_copy(0, qo, qg_hbm, h).start()

    def kv_finish(h):
        cols = slice(h * DK, (h + 1) * DK)
        base = sbd[h]
        for c in range(NC):
            r = slice(c * C, (c + 1) * C)
            back = base
            if c % 2 == 0:
                back = back + sgnode[h, c // 2]
            if (c // 2) % 2 == 0:
                back = back + sgnode[h, 4 + c // 4]
            if c < 4:
                back = back + sgnode[h, 6]
            hi, lo = split(back)
            ko[r, cols] += nt(v3[h, r, :], jnp.concatenate([hi, hi, lo], axis=1))
            wide = jnp.concatenate([hi, lo], axis=1)
            val = nn(k3[h, r, 0 : 2 * DK], jnp.concatenate([wide, wide], axis=0))
            vo[r, cols] += val[:, :DK] + val[:, DK:]
        out_copy(1, ko, kg_hbm, h).start()
        out_copy(2, vo, vg_hbm, h).start()

    def out_copy(i, src, dst, h):
        cols = pl.ds(h * DK, DK)
        return pltpu.make_async_copy(src.at[:, cols], dst.at[:, cols], out_sem.at[h, i])

    for h in range(HH):
        keys(h)
    pl.semaphore_wait(barrier, NX + NZ + NG - 3)
    a_start(0)

    @pl.when(xb[0] == 0)
    def _():
        p_copy().start()

    for h in range(HH):
        queries(h)
    w_load.wait()
    for level in (5, 4, 3):
        cotangent(level)
        a_start(level - 1)
    states_end()
    cotangent(2)
    a_start(1)
    cotangent(1)

    @pl.when(xb[0] == 1)
    def _():
        p_copy().start()

    fine(0)
    cotangents_end()
    fine(1)
    states_on(1)
    states_on(2)
    fine(2)
    states_on(3)
    near_states()
    fine(3)
    cotangents_on()
    coarse(0, 2)
    for j in range(1, NG):
        w_send(j).start()
    for item in (1, 2, 3):
        far_states(item)
    coarse(2, 3)
    for j in range(1, NG):
        l_send(j).start()
    for h in range(HH):
        q_finish(h)
    w_rcv[g] = w_src[g]
    l_rcv[g] = l_src[...]
    for j in range(1, NG):
        w_recv(j).wait_recv()
    total = w_rcv[0]
    for i in range(1, NG):
        total = total + w_rcv[i]
    w_fin[g] = total
    for j in range(1, NG):
        f_send(j).start()
    far_states(4)
    for h in range(HH):
        kv_finish(h)
    for j in range(1, NG):
        l_recv(j).wait_recv()
    late = l_rcv[0]
    for i in range(1, NG):
        late = late + l_rcv[i]
    for j in range(1, NG):
        f_recv(j).wait_recv()
    for i in range(NG):
        wo[:, i * C : (i + 1) * C] = w_fin[i]
    for n in range(3):
        for i in range(NG):
            wo[13 + n : 14 + n, i * C : (i + 1) * C] = late[n, i : i + 1, :]
    w_out = pltpu.make_async_copy(wo, wg_hbm, out_sem.at[HH, 0])
    w_out.start()

    for item in range(5):
        @pl.when(a_needed(item, x))
        def _():
            for j in range(1, NX):
                a_send(item, j).wait_send()

        for j in range(1, NX):
            @pl.when(c_needed(item, xpeer(j)))
            def _():
                c_send(item, j).wait_send()
    p_copy().wait_send()
    for to in range(NZ):
        @pl.when(z != to)
        def _():
            b_send(to, 0).wait_send()
    for j in range(1, NG):
        w_send(j).wait_send()
        f_send(j).wait_send()
        l_send(j).wait_send()
    for h in range(HH):
        out_copy(0, qo, qg_hbm, h).wait()
        out_copy(1, ko, kg_hbm, h).wait()
        out_copy(2, vo, vg_hbm, h).wait()
    w_out.wait()


def hand_out(*refs):
    ins, outs, sems = refs[:4], refs[4:8], refs[8]
    copies = [pltpu.make_async_copy(a, b, sems.at[i]) for i, (a, b) in enumerate(zip(ins, outs))]
    for copy in copies:
        copy.start()
    for copy in copies:
        copy.wait()


def local(query_rows, key_rows, value_rows, out_grad, level_weights):
    rows = (FR, HH * DK)
    dma = pltpu.SemaphoreType.DMA
    whole = jax.ShapeDtypeStruct(rows, F32)
    anywhere = pl.BlockSpec(memory_space=pl.ANY)
    wide = (HH, FR, 3 * DK)
    hbm = pl.BlockSpec(memory_space=pltpu.HBM)
    shapes = (whole, whole, whole, jax.ShapeDtypeStruct((16, FR), F32))
    grads = pl.pallas_call(
        kernel,
        out_shape=shapes,
        in_specs=[hbm] * 5,
        out_specs=(anywhere,) * 4,
        scratch_shapes=[
            pltpu.VMEM(rows, F32), pltpu.VMEM(rows, F32), pltpu.VMEM(rows, F32), pltpu.VMEM(rows, F32),
            pltpu.VMEM((16, FR), F32),
            pltpu.VMEM(rows, F32), pltpu.VMEM(rows, F32), pltpu.VMEM(rows, F32),
            pltpu.VMEM((16, FR), F32),
            pltpu.VMEM(wide, BF16), pltpu.VMEM(wide, BF16), pltpu.VMEM(wide, BF16), pltpu.VMEM(wide, BF16),
            pltpu.VMEM((HH, 2 * DK, FR), BF16),
            pltpu.VMEM((HH, DK, FR), F32),
            pltpu.VMEM((HH, DK, FR), F32),
            pltpu.VMEM((C, C), jnp.int32),
            pltpu.VMEM((HH, 7, DK, 3 * DK), BF16),
            pltpu.VMEM((HH, 7, DK, DK), F32),
            pltpu.VMEM((HH, 5 * DK, 3 * DK), BF16),
            pltpu.VMEM((HH, DK, DK), F32),
            pltpu.VMEM((6, HH, DK, DK), F32),
            pltpu.VMEM((5, NX, HH, PR, DK), F32),
            pltpu.VMEM((HH, DK, DK), F32),
            pltpu.VMEM((4, HH, PR, DK), F32),
            pltpu.VMEM((NZ, HH, PR, DK), F32),
            pltpu.VMEM((6, HH, PR, DK), F32),
            pltpu.VMEM((5, HH, DK, DK), F32),
            pltpu.VMEM((NC, 16, C), F32),
            pltpu.VMEM((NG, 16, C), F32),
            pltpu.VMEM((NG, 16, C), F32),
            pltpu.VMEM((3, NC, C), F32),
            pltpu.VMEM((NG, 3, NC, C), F32),
            dma((HH + 1, 4)), dma((HH + 1, 3)),
            dma((5, NX - 1)), dma((5, NX)),
            dma, dma,
            dma((NZ,)), dma((NZ,)),
            dma((5, NX - 1)), dma((5, NX)),
            dma((NG - 1,)), dma((NG,)),
            dma((NG - 1,)), dma((NG,)),
            dma((NG - 1,)), dma((NG,)),
        ],
        compiler_params=pltpu.CompilerParams(
            collective_id=0, has_side_effects=True, vmem_limit_bytes=101 * 512 * 1024
        ),
        name="tree_backward",
    )(query_rows, key_rows, value_rows, out_grad, level_weights)
    return pl.pallas_call(
        hand_out,
        out_shape=shapes,
        in_specs=[anywhere] * 4,
        out_specs=(hbm,) * 4,
        scratch_shapes=[dma((4,))],
        compiler_params=pltpu.CompilerParams(vmem_limit_bytes=1024 * 1024),
        name="hand_out",
    )(*grads)


def solution(mesh):
    in_specs = (P("tm", "head"), P("tm", "head"), P("tm", "head"), P("tm", "head"), P(None, "tm"))
    out_specs = (P("tm", "head"), P("tm", "head"), P("tm", "head"), P(None, "tm"))
    return jax.shard_map(local, mesh=mesh, in_specs=in_specs, out_specs=out_specs, check_vma=False)
```

time: 49.8 us -> 40.9 us (0.82)
  local copies, waits for them, and re-layouts: 6.82 us -> 0.83 us
  Pallas kernels: 42.1 us -> 39.3 us
    unnamed x10 -> x2, local copies, waits for them, and re-layouts: 6.82 us -> 0.83 us
    pallas_call x1 -> x2, Pallas kernels: 42.1 us -> 39.3 us  [the longest x1 37.6 us: local(): pl.pallas_call(kernel, out_shape=shapes, in_specs=[hbm] * 5, out_specs=(a...]
where the time goes in v1:
time: 40.9 us; the launch traced here: 40.8 us
  Pallas kernels  39.3 us (96%)
  local copies, waits for them, and re-layouts  0.83 us (2%)
  between operations  0.65 us (2%)
    pallas_call x1, Pallas kernels, local(): pl.pallas_call(kernel, out_shape=shapes, in_specs=[hbm] * 5, out_specs=(a...  37.6 us
    pallas_call x1, Pallas kernels, local(): pl.pallas_call(hand_out, out_shape=shapes, in_specs=[anywhere] * 4, out_s...  1.7 us
    unnamed x2, local copies, waits for them, and re-layouts  0.83 us

profile of v1, /device:TPU:1, one launch (start us, length us, event | category | flops | bytes accessed | tf_op | source)
XLA Modules:
  0.0 40.8 jit_solution(3255705864210942187)
XLA Ops:
  0.6 0.0 copy-start
  0.6 0.8 %copy-done = f32[16,1024]{1,0:T(8,128)S(1)} copy-done((f32[16,1024]{1,0:T(8,128)S(1)}, f32[16,1024]{1,0:T(8,128)}, u32[]{:S(2)}) %copy-start) | copy-done | bytes 65560
  1.5 37.6 %tree_backward.1 = (f32[1024,256]{1,0:T(8,128)S(1)}, f32[1024,256]{1,0:T(8,128)S(1)}, f32[1024,256]{1,0:T(8,128)S(1)}, f32[16,1024]{1,0:T(8,128)S(1)}) custom-call(f32[1024,256]{1,0:T(8,128)} %q_hbm.1, f32[1024,256]{1,0:T(8,128)} %k_hbm.1, f32[1024,256]{1,0:T(8,128)} %v_hbm.1, f32[1024,256]{1,0:T(8,128)} %d_hbm.1, f32[16,1024]{1,0:T(8,128)S(1)} %copy-done), custom_call_target="tpu_custom_call" | custom-call | tf_op jit(solution)/shard_map/tree_backward/pallas_call | solution.py:580
  39.1 1.7 %hand_out.1 = (f32[1024,256]{1,0:T(8,128)}, f32[1024,256]{1,0:T(8,128)}, f32[1024,256]{1,0:T(8,128)}, f32[16,1024]{1,0:T(8,128)}) custom-call(f32[1024,256]{1,0:T(8,128)S(1)} %get-tuple-element.8.refs_0_, f32[1024,256]{1,0:T(8,128)S(1)} %get-tuple-element.9.refs_1_, f32[1024,256]{1,0:T(8,128)S(1)} %get-tuple-element.10.refs_2_, ...), custom_call_target="tpu_custom_call" | custom-call | tf_op jit(solution)/shard_map/hand_out/pallas_call | solution.py:625
Async XLA Ops:
  0.6 0.8 %copy-start = (f32[16,1024]{1,0:T(8,128)S(1)}, f32[16,1024]{1,0:T(8,128)}, u32[]{:S(2)}) copy-start(f32[16,1024]{1,0:T(8,128)} %w_hbm.1) | copy-start | bytes 196612

commit v2 on v1

--- a/solution.py
+++ b/solution.py
@@ -335,10 +335,10 @@
         def _():
             b_src[0] = a_total(0)
 
-        for to in (7, 6, 5, 4, 3, 2, 1):
-            @pl.when(z < to)
+        for j in (4, 3, 5, 2, 6, 1, 7):
+            @pl.when(z + j < NZ)
             def _():
-                b_send(to, 0).start()
+                b_send(z + j, 0).start()
 
         c_src[0] = a_rcv[0, 0] + a_rcv[0, 1]
         c_start(0)
@@ -351,10 +351,10 @@
             def _():
                 b_src[1 + i] = a_total(2 + i)
 
-        for to in range(NZ - 1):
-            @pl.when(z > to)
+        for j in (4, 3, 5, 2, 6, 1, 7):
+            @pl.when(z - j >= 0)
             def _():
-                b_send(to, b_level(to)).start()
+                b_send(z - j, b_level(z - j)).start()
 
     def states_on(item):
         @pl.when(zb[item - 1] == 1)
@@ -477,7 +477,6 @@
     for level in (5, 4, 3):
         cotangent(level)
         a_start(level - 1)
-    states_end()
     cotangent(2)
     a_start(1)
     cotangent(1)
@@ -487,27 +486,22 @@
         p_copy().start()
 
     fine(0)
-    cotangents_end()
+    states_end()
     fine(1)
     states_on(1)
+    fine(2)
+    cotangents_end()
     states_on(2)
-    fine(2)
+    fine(3)
     states_on(3)
     near_states()
-    fine(3)
+    coarse(0, 2)
+    for j in range(1, NG):
+        w_send(j).start()
+    far_states(1)
+    far_states(2)
     cotangents_on()
-    coarse(0, 2)
-    for j in range(1, NG):
-        w_send(j).start()
-    for item in (1, 2, 3):
-        far_states(item)
-    coarse(2, 3)
-    for j in range(1, NG):
-        l_send(j).start()
-    for h in range(HH):
-        q_finish(h)
     w_rcv[g] = w_src[g]
-    l_rcv[g] = l_src[...]
     for j in range(1, NG):
         w_recv(j).wait_recv()
     total = w_rcv[0]
@@ -516,18 +510,25 @@
     w_fin[g] = total
     for j in range(1, NG):
         f_send(j).start()
+    far_states(3)
+    coarse(2, 3)
+    for j in range(1, NG):
+        l_send(j).start()
+    l_rcv[g] = l_src[...]
+    for h in range(HH):
+        q_finish(h)
     far_states(4)
     for h in range(HH):
         kv_finish(h)
+    for j in range(1, NG):
+        f_recv(j).wait_recv()
+    for i in range(NG):
+        wo[:, i * C : (i + 1) * C] = w_fin[i]
     for j in range(1, NG):
         l_recv(j).wait_recv()
     late = l_rcv[0]
     for i in range(1, NG):
         late = late + l_rcv[i]
-    for j in range(1, NG):
-        f_recv(j).wait_recv()
-    for i in range(NG):
-        wo[:, i * C : (i + 1) * C] = w_fin[i]
     for n in range(3):
         for i in range(NG):
             wo[13 + n : 14 + n, i * C : (i + 1) * C] = late[n, i : i + 1, :]
@@ -562,7 +563,12 @@
 
 def hand_out(*refs):
     ins, outs, sems = refs[:4], refs[4:8], refs[8]
-    copies = [pltpu.make_async_copy(a, b, sems.at[i]) for i, (a, b) in enumerate(zip(ins, outs))]
+    copies = []
+    for i in range(3):
+        for part in range(4):
+            r = pl.ds(part * (FR // 4), FR // 4)
+            copies.append(pltpu.make_async_copy(ins[i].at[r, :], outs[i].at[r, :], sems.at[4 * i + part]))
+    copies.append(pltpu.make_async_copy(ins[3], outs[3], sems.at[12]))
     for copy in copies:
         copy.start()
     for copy in copies:
@@ -627,7 +633,7 @@
         out_shape=shapes,
         in_specs=[anywhere] * 4,
         out_specs=(hbm,) * 4,
-        scratch_shapes=[dma((4,))],
+        scratch_shapes=[dma((13,))],
         compiler_params=pltpu.CompilerParams(vmem_limit_bytes=1024 * 1024),
         name="hand_out",
     )(*grads)

time: 40.9 us -> 38.6 us (0.944)
  Pallas kernels: 39.3 us -> 37 us
    pallas_call x1, Pallas kernels: 37.6 us -> 35.2 us  [local(): pl.pallas_call(kernel, out_shape=shapes, in_specs=[hbm] * 5, out_specs=(a...]
where the time goes in v2:
time: 38.6 us; the launch traced here: 38.5 us
  Pallas kernels  37 us (96%)
  local copies, waits for them, and re-layouts  0.83 us (2%)
  between operations  0.65 us (2%)
    pallas_call x1, Pallas kernels, local(): pl.pallas_call(kernel, out_shape=shapes, in_specs=[hbm] * 5, out_specs=(a...  35.2 us
    pallas_call x1, Pallas kernels, local(): pl.pallas_call(hand_out, out_shape=shapes, in_specs=[anywhere] * 4, out_s...  1.78 us
    unnamed x2, local copies, waits for them, and re-layouts  0.83 us

profile of v2, /device:TPU:1, one launch (start us, length us, event | category | flops | bytes accessed | tf_op | source)
XLA Modules:
  0.0 38.5 jit_solution(10657213848161075150)
XLA Ops:
  0.6 0.0 copy-start
  0.6 0.8 %copy-done = f32[16,1024]{1,0:T(8,128)S(1)} copy-done((f32[16,1024]{1,0:T(8,128)S(1)}, f32[16,1024]{1,0:T(8,128)}, u32[]{:S(2)}) %copy-start) | copy-done | bytes 65560
  1.5 35.2 %tree_backward.1 = (f32[1024,256]{1,0:T(8,128)S(1)}, f32[1024,256]{1,0:T(8,128)S(1)}, f32[1024,256]{1,0:T(8,128)S(1)}, f32[16,1024]{1,0:T(8,128)S(1)}) custom-call(f32[1024,256]{1,0:T(8,128)} %q_hbm.1, f32[1024,256]{1,0:T(8,128)} %k_hbm.1, f32[1024,256]{1,0:T(8,128)} %v_hbm.1, f32[1024,256]{1,0:T(8,128)} %d_hbm.1, f32[16,1024]{1,0:T(8,128)S(1)} %copy-done), custom_call_target="tpu_custom_call" | custom-call | tf_op jit(solution)/shard_map/tree_backward/pallas_call | solution.py:586
  36.7 1.8 %hand_out.1 = (f32[1024,256]{1,0:T(8,128)}, f32[1024,256]{1,0:T(8,128)}, f32[1024,256]{1,0:T(8,128)}, f32[16,1024]{1,0:T(8,128)}) custom-call(f32[1024,256]{1,0:T(8,128)S(1)} %get-tuple-element.8.refs_0_, f32[1024,256]{1,0:T(8,128)S(1)} %get-tuple-element.9.refs_1_, f32[1024,256]{1,0:T(8,128)S(1)} %get-tuple-element.10.refs_2_, ...), custom_call_target="tpu_custom_call" | custom-call | tf_op jit(solution)/shard_map/hand_out/pallas_call | solution.py:631
Async XLA Ops:
  0.6 0.8 %copy-start = (f32[16,1024]{1,0:T(8,128)S(1)}, f32[16,1024]{1,0:T(8,128)}, u32[]{:S(2)}) copy-start(f32[16,1024]{1,0:T(8,128)} %w_hbm.1) | copy-start | bytes 196612

commit v3 on v2

--- a/solution.py
+++ b/solution.py
@@ -77,11 +77,11 @@
         return pltpu.make_async_copy(src.at[:, cols], dst.at[:, cols], in_sem.at[h, i])
 
     w_load = pltpu.make_async_copy(w_hbm, win, in_sem.at[HH, 0])
-    for i in (0, 1):
+    for i in (2, 3):
         for h in range(HH):
             load(i, h).start()
     w_load.start()
-    for i in (2, 3):
+    for i in (0, 1):
         for h in range(HH):
             load(i, h).start()
 
@@ -148,13 +148,6 @@
 
     def b_recv(come):
         return remote(b_src.at[0], b_rcv.at[come], b_ss.at[come], b_rs.at[come], come * NX + x, g)
-
-    def b_level(to):
-        return (
-            1
-            + (lax.div(z, 2) != lax.div(to, 2)).astype(jnp.int32)
-            + (lax.div(z, 4) != lax.div(to, 4)).astype(jnp.int32)
-        )
 
     def c_needed(item, dst_x):
         if item == 0:
@@ -343,18 +336,15 @@
         c_src[0] = a_rcv[0, 0] + a_rcv[0, 1]
         c_start(0)
 
-    def cotangents_end():
-        for item in range(1, 5):
-            a_wait(item)
-        for i in range(3):
-            @pl.when(zb[i] == 1)
-            def _():
-                b_src[1 + i] = a_total(2 + i)
-
-        for j in (4, 3, 5, 2, 6, 1, 7):
-            @pl.when(z - j >= 0)
-            def _():
-                b_send(z - j, b_level(z - j)).start()
+    def cotangents_up(i):
+        @pl.when(zb[i] == 1)
+        def _():
+            a_wait(2 + i)
+            b_src[1 + i] = a_total(2 + i)
+            count = 1 << i
+            first = lax.div(z, count) * count - count
+            for k in range(count):
+                b_send(first + k, 1 + i).start()
 
     def states_on(item):
         @pl.when(zb[item - 1] == 1)
@@ -371,6 +361,7 @@
         c_start(item)
 
     def cotangents_on():
+        a_wait(1)
         c_src[5] = jnp.zeros((HH, PR, DK), F32)
         for other in range(1, NZ):
             @pl.when(other > z)
@@ -427,10 +418,7 @@
                 row = 11 + first + n
                 for sub in range(2):
                     part = terms[n][:, sub * C : (sub + 1) * C]
-                    if row < 13:
-                        w_src[2 * i + sub, row : row + 1, :] = part
-                    else:
-                        l_src[row - 13, 2 * i + sub : 2 * i + sub + 1, :] = part
+                    l_src[row - 11, 2 * i + sub : 2 * i + sub + 1, :] = part
 
     def q_finish(h):
         for c in range(NC):
@@ -463,44 +451,68 @@
         return pltpu.make_async_copy(src.at[:, cols], dst.at[:, cols], out_sem.at[h, i])
 
     for h in range(HH):
-        keys(h)
-    pl.semaphore_wait(barrier, NX + NZ + NG - 3)
-    a_start(0)
-
-    @pl.when(xb[0] == 0)
-    def _():
-        p_copy().start()
-
-    for h in range(HH):
         queries(h)
     w_load.wait()
-    for level in (5, 4, 3):
-        cotangent(level)
-        a_start(level - 1)
-    cotangent(2)
-    a_start(1)
-    cotangent(1)
-
-    @pl.when(xb[0] == 1)
+    cotangent(5)
+    low = z < NZ // 2
+
+    @pl.when(low)
     def _():
-        p_copy().start()
-
-    fine(0)
+        for level in (4, 3):
+            cotangent(level)
+        for h in range(HH):
+            keys(h)
+        for level in (2, 1):
+            cotangent(level)
+        fine(0)
+
+    pl.semaphore_wait(barrier, NX + NZ + NG - 3)
+
+    @pl.when(low)
+    def _():
+        for item in (0, 3, 2, 1):
+            a_start(item)
+
+    @pl.when(jnp.logical_not(low))
+    def _():
+        a_start(4)
+        for level in (4, 3):
+            cotangent(level)
+            a_start(level - 1)
+        for h in range(HH):
+            keys(h)
+        a_start(0)
+        cotangent(2)
+        a_start(1)
+        cotangent(1)
+        fine(0)
+        for i in (2, 1, 0):
+            cotangents_up(i)
+
+    fine(1)
     states_end()
-    fine(1)
+
+    @pl.when(low)
+    def _():
+        for i in (1, 0):
+            cotangents_up(i)
+
+    p_copy().start()
+    fine(2)
     states_on(1)
-    fine(2)
-    cotangents_end()
+    fine(3)
+    for j in range(1, NG):
+        w_send(j).start()
     states_on(2)
-    fine(3)
     states_on(3)
     near_states()
     coarse(0, 2)
-    for j in range(1, NG):
-        w_send(j).start()
-    far_states(1)
-    far_states(2)
     cotangents_on()
+    for item in (1, 2, 3):
+        far_states(item)
+    coarse(2, 3)
+    for j in range(1, NG):
+        l_send(j).start()
     w_rcv[g] = w_src[g]
     for j in range(1, NG):
         w_recv(j).wait_recv()
@@ -510,10 +522,6 @@
     w_fin[g] = total
     for j in range(1, NG):
         f_send(j).start()
-    far_states(3)
-    coarse(2, 3)
-    for j in range(1, NG):
-        l_send(j).start()
     l_rcv[g] = l_src[...]
     for h in range(HH):
         q_finish(h)
@@ -529,9 +537,9 @@
     late = l_rcv[0]
     for i in range(1, NG):
         late = late + l_rcv[i]
-    for n in range(3):
+    for n in range(5):
         for i in range(NG):
-            wo[13 + n : 14 + n, i * C : (i + 1) * C] = late[n, i : i + 1, :]
+            wo[11 + n : 12 + n, i * C : (i + 1) * C] = late[n, i : i + 1, :]
     w_out = pltpu.make_async_copy(wo, wg_hbm, out_sem.at[HH, 0])
     w_out.start()
 
@@ -612,8 +620,8 @@
             pltpu.VMEM((NC, 16, C), F32),
             pltpu.VMEM((NG, 16, C), F32),
             pltpu.VMEM((NG, 16, C), F32),
-            pltpu.VMEM((3, NC, C), F32),
-            pltpu.VMEM((NG, 3, NC, C), F32),
+            pltpu.VMEM((5, NC, C), F32),
+            pltpu.VMEM((NG, 5, NC, C), F32),
             dma((HH + 1, 4)), dma((HH + 1, 3)),
             dma((5, NX - 1)), dma((5, NX)),
             dma, dma,
@@ -627,7 +635,7 @@
             collective_id=0, has_side_effects=True, vmem_limit_bytes=101 * 512 * 1024
         ),
         name="tree_backward",
-    )(query_rows, key_rows, value_rows, out_grad, level_weights)
+    )(query_rows, key_rows, value_rows, out_grad, pltpu.with_memory_space_constraint(level_weights, pltpu.HBM))
     return pl.pallas_call(
         hand_out,
         out_shape=shapes,

time: 38.6 us -> 34.4 us (0.89)
  the two profiles are of different devices: /device:TPU:1 before, /device:TPU:97 now
where the time goes in v3:
time: 34.4 us; the launch traced here: 34.3 us
  Pallas kernels  33.5 us (97%)
  between operations  0.8 us (2%)
    pallas_call x1, Pallas kernels, local(): pl.pallas_call(kernel, out_shape=shapes, in_specs=[hbm] * 5, out_specs=(a...  31.7 us
    pallas_call x1, Pallas kernels, local(): pl.pallas_call(hand_out, out_shape=shapes, in_specs=[anywhere] * 4, out_s...  1.78 us

profile of v3, /device:TPU:97, one launch (start us, length us, event | category | flops | bytes accessed | tf_op | source)
XLA Modules:
  0.0 34.3 jit_solution(6818825317128408614)
XLA Ops:
  0.6 31.7 %tree_backward.1 = (f32[1024,256]{1,0:T(8,128)S(1)}, f32[1024,256]{1,0:T(8,128)S(1)}, f32[1024,256]{1,0:T(8,128)S(1)}, f32[16,1024]{1,0:T(8,128)S(1)}) custom-call(f32[1024,256]{1,0:T(8,128)} %q_hbm.1, f32[1024,256]{1,0:T(8,128)} %k_hbm.1, f32[1024,256]{1,0:T(8,128)} %v_hbm.1, f32[1024,256]{1,0:T(8,128)} %d_hbm.1, f32[16,1024]{1,0:T(8,128)} %w_hbm.1), custom_call_target="tpu_custom_call" | custom-call | tf_op jit(solution)/shard_map/tree_backward/pallas_call | solution.py:594
  32.3 1.8 %hand_out.1 = (f32[1024,256]{1,0:T(8,128)}, f32[1024,256]{1,0:T(8,128)}, f32[1024,256]{1,0:T(8,128)}, f32[16,1024]{1,0:T(8,128)}) custom-call(f32[1024,256]{1,0:T(8,128)S(1)} %get-tuple-element.8.refs_0_, f32[1024,256]{1,0:T(8,128)S(1)} %get-tuple-element.9.refs_1_, f32[1024,256]{1,0:T(8,128)S(1)} %get-tuple-element.10.refs_2_, ...), custom_call_target="tpu_custom_call" | custom-call | tf_op jit(solution)/shard_map/hand_out/pallas_call | solution.py:639

commit v4 on v3

--- a/solution.py
+++ b/solution.py
@@ -43,8 +43,8 @@
     q_hbm, k_hbm, v_hbm, d_hbm, w_hbm, qg_hbm, kg_hbm, vg_hbm, wg_hbm,
     qin, kin, vin, din, win, qo, ko, vo, wo,
     k3, v3, q3, d3, kt, qt, qgt, levels, snode, sgnode, sleft, sbd,
-    a_src, a_rcv, p_rcv, b_src, b_rcv, c_src, c_rcv, w_src, w_rcv, w_fin, l_src, l_rcv,
-    in_sem, out_sem, a_ss, a_rs, p_ss, p_rs, b_ss, b_rs, c_ss, c_rs, w_ss, w_rs, f_ss, f_rs, l_ss, l_rs,
+    a_src, a_rcv, p_rcv, b_src, b_rcv, c_src, c_rcv, w_src, w_rcv, w_sum, l_src, l_rcv, l_sum,
+    in_sem, out_sem, a_ss, a_rs, p_ss, p_rs, b_ss, b_rs, c_ss, c_rs, w_ss, w_rs, l_ss, l_rs,
 ):
     me = lax.axis_index("tm")
     g = lax.axis_index("head")
@@ -94,6 +94,7 @@
     levels[...] = jnp.where(source <= target, digits, -1)
     sleft[...] = jnp.zeros_like(sleft)
     w_src[...] = jnp.zeros_like(w_src)
+    l_src[...] = jnp.zeros_like(l_src)
     sbd[...] = jnp.zeros_like(sbd)
 
     def remote(src, dst, ss, rs, tm, head):
@@ -185,19 +186,11 @@
 
     def w_send(j):
         to = gpeer(j)
-        return remote(w_src.at[to], w_rcv.at[g], w_ss.at[j - 1], w_rs.at[g], me, to)
+        return remote(w_src, w_rcv.at[g], w_ss.at[j - 1], w_rs.at[g], me, to)
 
     def w_recv(j):
         come = gpeer(j)
-        return remote(w_src.at[come], w_rcv.at[come], w_ss.at[j - 1], w_rs.at[come], me, come)
-
-    def f_send(j):
-        to = gpeer(j)
-        return remote(w_fin.at[g], w_fin.at[g], f_ss.at[j - 1], f_rs.at[g], me, to)
-
-    def f_recv(j):
-        come = gpeer(j)
-        return remote(w_fin.at[come], w_fin.at[come], f_ss.at[j - 1], f_rs.at[come], me, come)
+        return remote(w_src, w_rcv.at[come], w_ss.at[j - 1], w_rs.at[come], me, come)
 
     def l_send(j):
         to = gpeer(j)
@@ -291,7 +284,8 @@
             rows = [
                 jnp.sum(jnp.where(level == k, product, F32(0.0)), axis=0, keepdims=True) for k in range(8)
             ]
-            w_src[c, 0:8, :] = jnp.concatenate(rows, axis=0)
+            for k in range(8):
+                w_src[k, c : c + 1, :] = rows[k]
         terms = {}
         for h in range(HH):
             for lev, node, r, along in along_of[h]:
@@ -316,10 +310,10 @@
                 qgt[h, :, c * C : (c + 1) * C] = q_parts[h][sub]
         for lev, term in terms.items():
             if lev == 8:
-                w_src[2 * i + 1, 8:9, :] = term
+                w_src[8, 2 * i + 1 : 2 * i + 2, :] = term
             else:
-                w_src[2 * i, lev : lev + 1, :] = term[:, :C]
-                w_src[2 * i + 1, lev : lev + 1, :] = term[:, C:]
+                w_src[lev, 2 * i : 2 * i + 1, :] = term[:, :C]
+                w_src[lev, 2 * i + 1 : 2 * i + 2, :] = term[:, C:]
 
     def states_end():
         a_wait(0)
@@ -400,6 +394,7 @@
             else:
                 for h in range(HH):
                     sleft[h, (item + 1) * DK : (item + 2) * DK, :] = as_left(c_rcv[item, h])
+                coarse(item + 1, 1)
 
     def coarse(first, count):
         for i in range(FR // (2 * C)):
@@ -503,46 +498,34 @@
     fine(3)
     for j in range(1, NG):
         w_send(j).start()
+    w_rcv[g] = w_src[...]
     states_on(2)
     states_on(3)
     near_states()
     coarse(0, 2)
+    for item in (1, 2):
+        far_states(item)
     cotangents_on()
-    for item in (1, 2, 3):
-        far_states(item)
-    coarse(2, 3)
+    far_states(3)
     for j in range(1, NG):
         l_send(j).start()
-    w_rcv[g] = w_src[g]
-    for j in range(1, NG):
-        w_recv(j).wait_recv()
-    total = w_rcv[0]
-    for i in range(1, NG):
-        total = total + w_rcv[i]
-    w_fin[g] = total
-    for j in range(1, NG):
-        f_send(j).start()
     l_rcv[g] = l_src[...]
     for h in range(HH):
         q_finish(h)
     far_states(4)
     for h in range(HH):
         kv_finish(h)
-    for j in range(1, NG):
-        f_recv(j).wait_recv()
-    for i in range(NG):
-        wo[:, i * C : (i + 1) * C] = w_fin[i]
-    for j in range(1, NG):
-        l_recv(j).wait_recv()
-    late = l_rcv[0]
-    for i in range(1, NG):
-        late = late + l_rcv[i]
-    for n in range(5):
-        for i in range(NG):
-            wo[11 + n : 12 + n, i * C : (i + 1) * C] = late[n, i : i + 1, :]
-    w_out = pltpu.make_async_copy(wo, wg_hbm, out_sem.at[HH, 0])
-    w_out.start()
-
+    def gather(src, dst, first, last, recv):
+        for j in range(1, NG):
+            recv(j).wait_recv()
+        total = src[0]
+        for i in range(1, NG):
+            total = total + src[i]
+        dst[...] = total
+        for i in range(NC):
+            wo[first:last, i * C : (i + 1) * C] = dst[:, i, :]
+
+    gather(w_rcv, w_sum, 0, 11, w_recv)
     for item in range(5):
         @pl.when(a_needed(item, x))
         def _():
@@ -560,12 +543,15 @@
             b_send(to, 0).wait_send()
     for j in range(1, NG):
         w_send(j).wait_send()
-        f_send(j).wait_send()
-        l_send(j).wait_send()
     for h in range(HH):
         out_copy(0, qo, qg_hbm, h).wait()
         out_copy(1, ko, kg_hbm, h).wait()
         out_copy(2, vo, vg_hbm, h).wait()
+    gather(l_rcv, l_sum, 11, 16, l_recv)
+    w_out = pltpu.make_async_copy(wo, wg_hbm, out_sem.at[HH, 0])
+    w_out.start()
+    for j in range(1, NG):
+        l_send(j).wait_send()
     w_out.wait()
 
 
@@ -617,17 +603,17 @@
             pltpu.VMEM((NZ, HH, PR, DK), F32),
             pltpu.VMEM((6, HH, PR, DK), F32),
             pltpu.VMEM((5, HH, DK, DK), F32),
-            pltpu.VMEM((NC, 16, C), F32),
-            pltpu.VMEM((NG, 16, C), F32),
-            pltpu.VMEM((NG, 16, C), F32),
+            pltpu.VMEM((11, NC, C), F32),
+            pltpu.VMEM((NG, 11, NC, C), F32),
+            pltpu.VMEM((11, NC, C), F32),
             pltpu.VMEM((5, NC, C), F32),
             pltpu.VMEM((NG, 5, NC, C), F32),
+            pltpu.VMEM((5, NC, C), F32),
             dma((HH + 1, 4)), dma((HH + 1, 3)),
             dma((5, NX - 1)), dma((5, NX)),
             dma, dma,
             dma((NZ,)), dma((NZ,)),
             dma((5, NX - 1)), dma((5, NX)),
-            dma((NG - 1,)), dma((NG,)),
             dma((NG - 1,)), dma((NG,)),
             dma((NG - 1,)), dma((NG,)),
         ],

time: 34.4 us -> 32.8 us (0.953)
  Pallas kernels: 33.5 us -> 31.9 us
    pallas_call x1, Pallas kernels: 31.7 us -> 30.1 us  [local(): pl.pallas_call(kernel, out_shape=shapes, in_specs=[hbm] * 5, out_specs=(a...]
where the time goes in v4:
time: 32.8 us; the launch traced here: 32.7 us
  Pallas kernels  31.9 us (97%)
  between operations  0.8 us (2%)
    pallas_call x1, Pallas kernels, local(): pl.pallas_call(kernel, out_shape=shapes, in_specs=[hbm] * 5, out_specs=(a...  30.1 us
    pallas_call x1, Pallas kernels, local(): pl.pallas_call(hand_out, out_shape=shapes, in_specs=[anywhere] * 4, out_s...  1.78 us

profile of v4, /device:TPU:97, one launch (start us, length us, event | category | flops | bytes accessed | tf_op | source)
XLA Modules:
  0.0 32.7 jit_solution(2891388977807540072)
XLA Ops:
  0.6 30.1 %tree_backward.1 = (f32[1024,256]{1,0:T(8,128)S(1)}, f32[1024,256]{1,0:T(8,128)S(1)}, f32[1024,256]{1,0:T(8,128)S(1)}, f32[16,1024]{1,0:T(8,128)S(1)}) custom-call(f32[1024,256]{1,0:T(8,128)} %q_hbm.1, f32[1024,256]{1,0:T(8,128)} %k_hbm.1, f32[1024,256]{1,0:T(8,128)} %v_hbm.1, f32[1024,256]{1,0:T(8,128)} %d_hbm.1, f32[16,1024]{1,0:T(8,128)} %w_hbm.1), custom_call_target="tpu_custom_call" | custom-call | tf_op jit(solution)/shard_map/tree_backward/pallas_call | solution.py:580
  30.7 1.8 %hand_out.1 = (f32[1024,256]{1,0:T(8,128)}, f32[1024,256]{1,0:T(8,128)}, f32[1024,256]{1,0:T(8,128)}, f32[16,1024]{1,0:T(8,128)}) custom-call(f32[1024,256]{1,0:T(8,128)S(1)} %get-tuple-element.8.refs_0_, f32[1024,256]{1,0:T(8,128)S(1)} %get-tuple-element.9.refs_1_, f32[1024,256]{1,0:T(8,128)S(1)} %get-tuple-element.10.refs_2_, ...), custom_call_target="tpu_custom_call" | custom-call | tf_op jit(solution)/shard_map/hand_out/pallas_call | solution.py:625

commit v5 on v4

--- a/solution.py
+++ b/solution.py
@@ -53,6 +53,7 @@
     xb = (lax.rem(x, 2), lax.div(x, 2))
     zb = (lax.rem(z, 2), lax.rem(lax.div(z, 2), 2), lax.div(z, 4))
     bits = xb + zb
+    low = z < NZ // 2
 
     def xpeer(j):
         return lax.rem(x + j, NX)
@@ -322,10 +323,15 @@
         def _():
             b_src[0] = a_total(0)
 
-        for j in (4, 3, 5, 2, 6, 1, 7):
-            @pl.when(z + j < NZ)
+        for j in (1, 2, 3):
+            @pl.when(lax.rem(z, 4) + j < 4)
             def _():
                 b_send(z + j, 0).start()
+
+        @pl.when(low)
+        def _():
+            for to in (7, 6, 5, 4):
+                b_send(to, 0).start()
 
         c_src[0] = a_rcv[0, 0] + a_rcv[0, 1]
         c_start(0)
@@ -337,7 +343,7 @@
             b_src[1 + i] = a_total(2 + i)
             count = 1 << i
             first = lax.div(z, count) * count - count
-            for k in range(count):
+            for k in reversed(range(count)):
                 b_send(first + k, 1 + i).start()
 
     def states_on(item):
@@ -449,7 +455,6 @@
         queries(h)
     w_load.wait()
     cotangent(5)
-    low = z < NZ // 2
 
     @pl.when(low)
     def _():
@@ -503,9 +508,9 @@
     states_on(3)
     near_states()
     coarse(0, 2)
-    for item in (1, 2):
-        far_states(item)
+    far_states(1)
     cotangents_on()
+    far_states(2)
     far_states(3)
     for j in range(1, NG):
         l_send(j).start()

time: 32.8 us -> 32.5 us (level)
  no operation moved by 1% of the time
where the time goes in v5:
time: 32.5 us; the launch traced here: 32.4 us
  Pallas kernels  31.6 us (97%)
  between operations  0.8 us (2%)
    pallas_call x1, Pallas kernels, local(): pl.pallas_call(kernel, out_shape=shapes, in_specs=[hbm] * 5, out_specs=(a...  29.9 us
    pallas_call x1, Pallas kernels, local(): pl.pallas_call(hand_out, out_shape=shapes, in_specs=[anywhere] * 4, out_s...  1.78 us

profile of v5, /device:TPU:97, one launch (start us, length us, event | category | flops | bytes accessed | tf_op | source)
XLA Modules:
  0.0 32.4 jit_solution(14841540136461895056)
XLA Ops:
  0.6 29.9 %tree_backward.1 = (f32[1024,256]{1,0:T(8,128)S(1)}, f32[1024,256]{1,0:T(8,128)S(1)}, f32[1024,256]{1,0:T(8,128)S(1)}, f32[16,1024]{1,0:T(8,128)S(1)}) custom-call(f32[1024,256]{1,0:T(8,128)} %q_hbm.1, f32[1024,256]{1,0:T(8,128)} %k_hbm.1, f32[1024,256]{1,0:T(8,128)} %v_hbm.1, f32[1024,256]{1,0:T(8,128)} %d_hbm.1, f32[16,1024]{1,0:T(8,128)} %w_hbm.1), custom_call_target="tpu_custom_call" | custom-call | tf_op jit(solution)/shard_map/tree_backward/pallas_call | solution.py:585
  30.5 1.8 %hand_out.1 = (f32[1024,256]{1,0:T(8,128)}, f32[1024,256]{1,0:T(8,128)}, f32[1024,256]{1,0:T(8,128)}, f32[16,1024]{1,0:T(8,128)}) custom-call(f32[1024,256]{1,0:T(8,128)S(1)} %get-tuple-element.8.refs_0_, f32[1024,256]{1,0:T(8,128)S(1)} %get-tuple-element.9.refs_1_, f32[1024,256]{1,0:T(8,128)S(1)} %get-tuple-element.10.refs_2_, ...), custom_call_target="tpu_custom_call" | custom-call | tf_op jit(solution)/shard_map/hand_out/pallas_call | solution.py:630

commit v6 on v5

--- a/solution.py
+++ b/solution.py
@@ -500,11 +500,20 @@
     p_copy().start()
     fine(2)
     states_on(1)
+
+    @pl.when(low)
+    def _():
+        states_on(2)
+
     fine(3)
     for j in range(1, NG):
         w_send(j).start()
     w_rcv[g] = w_src[...]
-    states_on(2)
+
+    @pl.when(jnp.logical_not(low))
+    def _():
+        states_on(2)
+
     states_on(3)
     near_states()
     coarse(0, 2)

time: 32.5 us -> 32.4 us (level)
  the two profiles are of different devices: /device:TPU:97 before, /device:TPU:1 now
where the time goes in v6:
time: 32.4 us; the launch traced here: 31.8 us
  Pallas kernels  31 us (96%)
  between operations  0.8 us (2%)
    pallas_call x1, Pallas kernels, local(): pl.pallas_call(kernel, out_shape=shapes, in_specs=[hbm] * 5, out_specs=(a...  29.2 us
    pallas_call x1, Pallas kernels, local(): pl.pallas_call(hand_out, out_shape=shapes, in_specs=[anywhere] * 4, out_s...  1.78 us

profile of v6, /device:TPU:1, one launch (start us, length us, event | category | flops | bytes accessed | tf_op | source)
XLA Modules:
  0.0 31.8 jit_solution(3394057100802779597)
XLA Ops:
  0.6 29.2 %tree_backward.1 = (f32[1024,256]{1,0:T(8,128)S(1)}, f32[1024,256]{1,0:T(8,128)S(1)}, f32[1024,256]{1,0:T(8,128)S(1)}, f32[16,1024]{1,0:T(8,128)S(1)}) custom-call(f32[1024,256]{1,0:T(8,128)} %q_hbm.1, f32[1024,256]{1,0:T(8,128)} %k_hbm.1, f32[1024,256]{1,0:T(8,128)} %v_hbm.1, f32[1024,256]{1,0:T(8,128)} %d_hbm.1, f32[16,1024]{1,0:T(8,128)} %w_hbm.1), custom_call_target="tpu_custom_call" | custom-call | tf_op jit(solution)/shard_map/tree_backward/pallas_call | solution.py:594
  29.9 1.8 %hand_out.1 = (f32[1024,256]{1,0:T(8,128)}, f32[1024,256]{1,0:T(8,128)}, f32[1024,256]{1,0:T(8,128)}, f32[16,1024]{1,0:T(8,128)}) custom-call(f32[1024,256]{1,0:T(8,128)S(1)} %get-tuple-element.8.refs_0_, f32[1024,256]{1,0:T(8,128)S(1)} %get-tuple-element.9.refs_1_, f32[1024,256]{1,0:T(8,128)S(1)} %get-tuple-element.10.refs_2_, ...), custom_call_target="tpu_custom_call" | custom-call | tf_op jit(solution)/shard_map/hand_out/pallas_call | solution.py:639
